TPU v7x, 32 devices: a whole 2x2x4 slice. The times are simulated.
32 devices in a mesh: clip: 4 (over z), ha: 4 (over y, x), wa: 2 (over core).
Axes of the slice: x: 2, y: 2, z: 4, core: 2. Of those that a mesh axis runs over, the one named last changes fastest.
Arguments:
- slow_in: float32 [4, 8, 16, 16, 1024], P('clip', None, 'ha', 'wa'), may hold values from -6 to 6
- fast_in: float32 [4, 32, 16, 16, 128], P('clip', None, 'ha', 'wa'), may hold values from -6 to 6
- valid_frames: int32 [4], replicated, may hold values from 1 to 8, as said below
- lateral_w: bfloat16 [2, 5, 128, 256], replicated, may hold values from -0.25 to 0.25
- slow_temporal_w: bfloat16 [2, 3, 1280, 256], replicated, may hold values from -0.09375 to 0.09375
- slow_spatial_w: bfloat16 [2, 3, 3, 256, 256], replicated, may hold values from -0.125 to 0.125
- slow_expand_w: bfloat16 [2, 256, 1024], replicated, may hold values from -0.375 to 0.375
- slow_skip_w: bfloat16 [2, 1280, 1024], replicated, may hold values from -0.15625 to 0.15625
- fast_temporal_w: bfloat16 [2, 3, 128, 32], replicated, may hold values from -0.3125 to 0.3125
- fast_spatial_w: bfloat16 [2, 3, 3, 32, 32], replicated, may hold values from -0.375 to 0.375
- fast_expand_w: bfloat16 [2, 32, 128], replicated, may hold values from -1 to 1
- fast_skip_w: bfloat16 [2, 128, 128], replicated, may hold values from -0.5 to 0.5
- gains: float32 [2, 3136], replicated, may hold values from 0.25 to 1.75
- biases: float32 [2, 3136], replicated, may hold values from -1.5 to 1.5
- slow_cot: float32 [4, 8, 16, 16, 1024], P('clip', None, 'ha', 'wa'), may hold values from -6 to 6
- fast_cot: float32 [4, 32, 16, 16, 128], P('clip', None, 'ha', 'wa'), may hold values from -6 to 6
Outputs:
- out_slow: float32 [4, 8, 16, 16, 1024], P('clip', None, 'ha', 'wa')
- out_fast: float32 [4, 32, 16, 16, 128], P('clip', None, 'ha', 'wa')
- grad_slow_in: float32 [4, 8, 16, 16, 1024], P('clip', None, 'ha', 'wa')
- grad_fast_in: float32 [4, 32, 16, 16, 128], P('clip', None, 'ha', 'wa')
- grad_lateral_w: float32 [2, 5, 128, 256], P(None, None, ('ha', 'wa'), 'clip')
- grad_slow_temporal_w: float32 [2, 3, 1280, 256], P(None, None, ('ha', 'wa'), 'clip')
- grad_slow_spatial_w: float32 [2, 3, 3, 256, 256], P(None, None, None, ('ha', 'wa'), 'clip')
- grad_slow_expand_w: float32 [2, 256, 1024], P(None, ('ha', 'wa'), 'clip')
- grad_slow_skip_w: float32 [2, 1280, 1024], P(None, ('ha', 'wa'), 'clip')
- grad_fast_temporal_w: float32 [2, 3, 128, 32], P(None, None, ('ha', 'wa'), 'clip')
- grad_fast_spatial_w: float32 [2, 3, 3, 32, 32], P(None, None, None, ('ha', 'wa'), 'clip')
- grad_fast_expand_w: float32 [2, 32, 128], P(None, ('ha', 'wa'), 'clip')
- grad_fast_skip_w: float32 [2, 128, 128], P(None, ('ha', 'wa'), 'clip')
- grad_gains: float32 [2, 3136], replicated
- grad_biases: float32 [2, 3136], replicated
Inputs may be any that keep to these rules, and one draw needn't show every extreme that they name: valid_frames[c] sets the masks and counts of the steps for clip c; the last clip has all 8.
All inputs are finite; a program needn't handle non-finite values.
Results may differ from a plain program's by a relative error of at most 0.024.
Values may be sent and summed in bfloat16 or wider, within the bound.
No kernel may reach another device: no remote copies, remote signals or barrier semaphores. Data moves between devices by JAX's collectives and lax.ppermute only.
A program may use at most 256 MiB of HBM per device.

v0:
```python
import jax
import jax.numpy as jnp
from jax import lax
from jax.sharding import PartitionSpec as P

DS = 1024
DL = 256
BS = 256
DF = 128
BF = 32
ST = 8
ALPHA = 4
HT = 16
WD = 16
LAYERS = 2


EPSILON = 1e-05


def with_halo(shard, sides, width):
    for axis, dim in sides:
        count, length = (lax.axis_size(axis), shard.shape[dim])
        up = [(i, (i + 1) % count) for i in range(count - 1)]
        down = [(j, i) for i, j in up]
        last = lax.slice_in_dim(shard, length - width, length, axis=dim)
        leading = lax.slice_in_dim(shard, 0, width, axis=dim)
        before = lax.ppermute(last, axis, up)
        after = lax.ppermute(leading, axis, down)
        shard = jnp.concatenate([before, shard, after], axis=dim)
    return shard


def for_sending(shard):

    def short(part):
        return part.astype(jnp.bfloat16) if part.dtype == jnp.float32 else part

    return jax.tree.map(short, shard)


def swish_unit(values):
    return values * jax.nn.sigmoid(values)


def swish_slope(values):
    sigma = jax.nn.sigmoid(values)
    return sigma * (1.0 + values * (1.0 - sigma))


def split_norms(vector):
    pieces = []
    offset = 0
    for column_count in [DL, BS, BS, DS, DS, BF, BF, DF, DF]:
        pieces.append(vector[offset : offset + column_count])
        offset += column_count
    return pieces


def apply_weight(inputs, weight):
    return jnp.einsum("...k,kn->...n", inputs, weight, preferred_element_type=jnp.float32)


def apply_back(gradient, weight):
    return jnp.einsum("...n,kn->...k", gradient, weight, preferred_element_type=jnp.float32)


def weight_grad(inputs, gradient):
    rows_in = inputs.reshape(-1, inputs.shape[-1])
    rows_out = gradient.reshape(-1, gradient.shape[-1])
    return jnp.einsum("rk,rn->kn", rows_in, rows_out, preferred_element_type=jnp.float32)


def time_taps(values):
    frames = values.shape[1]
    padded = jnp.pad(values, ((0, 0), (1, 1), (0, 0), (0, 0), (0, 0)))
    return jnp.concatenate(
        [padded[:, 0:frames], padded[:, 1 : frames + 1], padded[:, 2 : frames + 2]], axis=-1
    )


def time_untaps(gradient, column_count):
    before = gradient[..., :column_count]
    centre = gradient[..., column_count : 2 * column_count]
    later_tap = gradient[..., 2 * column_count :]
    zero_frame = jnp.zeros_like(centre[:, :1])
    return (
        centre
        + jnp.concatenate([before[:, 1:], zero_frame], axis=1)
        + jnp.concatenate([zero_frame, later_tap[:, :-1]], axis=1)
    )


def lateral_taps(values):
    frames = values.shape[1] // ALPHA
    padded = jnp.pad(values, ((0, 0), (2, 2), (0, 0), (0, 0), (0, 0)))
    return jnp.concatenate([padded[:, k : k + ALPHA * frames : ALPHA] for k in range(5)], axis=-1)


def lateral_untaps(gradient, column_count):
    frames = gradient.shape[1]
    target = jnp.zeros(
        (gradient.shape[0], ALPHA * frames + 4, gradient.shape[2], gradient.shape[3], column_count),
        jnp.float32,
    )
    for k in range(5):
        target = target.at[:, k : k + ALPHA * frames : ALPHA].add(
            gradient[..., k * column_count : (k + 1) * column_count]
        )
    return target[:, 2 : 2 + ALPHA * frames]


def pixel_taps(padded):
    height = padded.shape[2] - 2
    breadth = padded.shape[3] - 2
    return jnp.concatenate(
        [padded[:, :, a : a + height, b : b + breadth] for a in range(3) for b in range(3)], axis=-1
    )


def pixel_back(padded, weight):
    height = padded.shape[2] - 2
    breadth = padded.shape[3] - 2
    stacked = jnp.concatenate(
        [
            padded[:, :, 2 - a : 2 - a + height, 2 - b : 2 - b + breadth]
            for a in range(3)
            for b in range(3)
        ],
        axis=-1,
    )
    turned = jnp.transpose(weight, (0, 1, 3, 2)).reshape(-1, weight.shape[2])
    return apply_weight(stacked, turned)


def pixel_rim(values):
    return with_halo(values, (("ha", 2), ("wa", 3)), 1)


def grad_rim(values):
    return with_halo(values, (("ha", 2), ("wa", 3)), 1)


def local_moments(values, mask_vals):
    masked = values * mask_vals
    return jnp.stack(
        [jnp.sum(masked, axis=(0, 1, 2, 3)), jnp.sum(masked * values, axis=(0, 1, 2, 3))]
    )


def local_back(gradient, normed):
    return jnp.stack(
        [jnp.sum(gradient, axis=(0, 1, 2, 3)), jnp.sum(gradient * normed, axis=(0, 1, 2, 3))]
    )


def moment_totals(term_list):
    return [lax.psum(one_term, ("clip", "ha", "wa")) for one_term in term_list]


def grad_totals(term_list):
    return [lax.psum(one_term, ("clip", "ha", "wa")) for one_term in term_list]


def normalize(values, totals, count_all, gain_part, bias_part):
    centre = totals[0] / count_all
    inv_std = lax.rsqrt(totals[1] / count_all - centre * centre + EPSILON)
    normed = (values - centre) * inv_std
    return (gain_part * normed + bias_part, normed, inv_std)


def norm_back(gradient, normed, inv_std, gain_part, mask_vals, count_all, totals):
    return (
        gain_part * inv_std * (gradient - mask_vals * (totals[0] + normed * totals[1]) / count_all)
    ).astype(jnp.bfloat16)


def block_forward(
    slow_act,
    fast_act,
    weights,
    gain_parts,
    bias_parts,
    mask_slow,
    mask_fast,
    count_slow,
    count_fast,
):
    (
        lateral_w,
        slow_temporal_w,
        slow_spatial_w,
        slow_expand_w,
        slow_skip_w,
        fast_temporal_w,
        fast_spatial_w,
        fast_expand_w,
        fast_skip_w,
    ) = weights
    fast_low = fast_act.astype(jnp.bfloat16)
    lateral_pre = apply_weight(lateral_taps(fast_low), lateral_w.reshape(-1, DL))
    fast_temporal_pre = apply_weight(time_taps(fast_low), fast_temporal_w.reshape(-1, BF))
    fast_skip_pre = apply_weight(fast_low, fast_skip_w)
    totals_one = moment_totals(
        [
            local_moments(lateral_pre, mask_slow),
            local_moments(fast_temporal_pre, mask_fast),
            local_moments(fast_skip_pre, mask_fast),
        ]
    )
    lateral_out = normalize(lateral_pre, totals_one[0], count_slow, gain_parts[0], bias_parts[0])
    fast_temporal_out = normalize(
        fast_temporal_pre, totals_one[1], count_fast, gain_parts[5], bias_parts[5]
    )
    fast_skip_out = normalize(
        fast_skip_pre, totals_one[2], count_fast, gain_parts[8], bias_parts[8]
    )
    cat_low = jnp.concatenate(
        [slow_act.astype(jnp.bfloat16), swish_unit(lateral_out[0]).astype(jnp.bfloat16)], axis=-1
    )
    slow_temporal_pre = apply_weight(time_taps(cat_low), slow_temporal_w.reshape(-1, BS))
    slow_skip_pre = apply_weight(cat_low, slow_skip_w)
    fast_mid_pad = pixel_rim(swish_unit(fast_temporal_out[0]).astype(jnp.bfloat16))
    fast_spatial_pre = apply_weight(pixel_taps(fast_mid_pad), fast_spatial_w.reshape(-1, BF))
    totals_two = moment_totals(
        [
            local_moments(slow_temporal_pre, mask_slow),
            local_moments(slow_skip_pre, mask_slow),
            local_moments(fast_spatial_pre, mask_fast),
        ]
    )
    slow_temporal_out = normalize(
        slow_temporal_pre, totals_two[0], count_slow, gain_parts[1], bias_parts[1]
    )
    slow_skip_out = normalize(
        slow_skip_pre, totals_two[1], count_slow, gain_parts[4], bias_parts[4]
    )
    fast_spatial_out = normalize(
        fast_spatial_pre, totals_two[2], count_fast, gain_parts[6], bias_parts[6]
    )
    slow_mid_pad = pixel_rim(swish_unit(slow_temporal_out[0]).astype(jnp.bfloat16))
    slow_spatial_pre = apply_weight(pixel_taps(slow_mid_pad), slow_spatial_w.reshape(-1, BS))
    fast_top_low = swish_unit(fast_spatial_out[0]).astype(jnp.bfloat16)
    fast_expand_pre = apply_weight(fast_top_low, fast_expand_w)
    totals_three = moment_totals(
        [local_moments(slow_spatial_pre, mask_slow), local_moments(fast_expand_pre, mask_fast)]
    )
    slow_spatial_out = normalize(
        slow_spatial_pre, totals_three[0], count_slow, gain_parts[2], bias_parts[2]
    )
    fast_expand_out = normalize(
        fast_expand_pre, totals_three[1], count_fast, gain_parts[7], bias_parts[7]
    )
    slow_top_low = swish_unit(slow_spatial_out[0]).astype(jnp.bfloat16)
    slow_expand_pre = apply_weight(slow_top_low, slow_expand_w)
    totals_four = moment_totals([local_moments(slow_expand_pre, mask_slow)])
    slow_expand_out = normalize(
        slow_expand_pre, totals_four[0], count_slow, gain_parts[3], bias_parts[3]
    )
    slow_sum = slow_expand_out[0] + slow_skip_out[0]
    fast_sum = fast_expand_out[0] + fast_skip_out[0]
    stored = {
        "fast_low": fast_low,
        "cat_low": cat_low,
        "lateral": lateral_out,
        "slow_temporal": slow_temporal_out,
        "slow_spatial": slow_spatial_out,
        "slow_expand": slow_expand_out,
        "slow_skip": slow_skip_out,
        "fast_temporal": fast_temporal_out,
        "fast_spatial": fast_spatial_out,
        "fast_expand": fast_expand_out,
        "fast_skip": fast_skip_out,
        "slow_mid_pad": slow_mid_pad,
        "fast_mid_pad": fast_mid_pad,
        "slow_top_low": slow_top_low,
        "fast_top_low": fast_top_low,
        "slow_sum": slow_sum,
        "fast_sum": fast_sum,
    }
    return (mask_slow * swish_unit(slow_sum), mask_fast * swish_unit(fast_sum), stored)


def block_backward(
    grad_slow, grad_fast, stored, weights, gain_parts, mask_slow, mask_fast, count_slow, count_fast
):
    (
        lateral_w,
        slow_temporal_w,
        slow_spatial_w,
        slow_expand_w,
        slow_skip_w,
        fast_temporal_w,
        fast_spatial_w,
        fast_expand_w,
        fast_skip_w,
    ) = weights
    fast_low = stored["fast_low"]
    cat_low = stored["cat_low"]
    lateral_out = stored["lateral"]
    slow_temporal_out = stored["slow_temporal"]
    slow_spatial_out = stored["slow_spatial"]
    slow_expand_out = stored["slow_expand"]
    slow_skip_out = stored["slow_skip"]
    fast_temporal_out = stored["fast_temporal"]
    fast_spatial_out = stored["fast_spatial"]
    fast_expand_out = stored["fast_expand"]
    fast_skip_out = stored["fast_skip"]
    slow_final = grad_slow * mask_slow * swish_slope(stored["slow_sum"])
    fast_final = grad_fast * mask_fast * swish_slope(stored["fast_sum"])
    totals_one = grad_totals(
        [
            local_back(slow_final, slow_expand_out[1]),
            local_back(slow_final, slow_skip_out[1]),
            local_back(fast_final, fast_expand_out[1]),
            local_back(fast_final, fast_skip_out[1]),
        ]
    )
    slow_expand_grad = norm_back(
        slow_final,
        slow_expand_out[1],
        slow_expand_out[2],
        gain_parts[3],
        mask_slow,
        count_slow,
        totals_one[0],
    )
    slow_skip_grad = norm_back(
        slow_final,
        slow_skip_out[1],
        slow_skip_out[2],
        gain_parts[4],
        mask_slow,
        count_slow,
        totals_one[1],
    )
    fast_expand_grad = norm_back(
        fast_final,
        fast_expand_out[1],
        fast_expand_out[2],
        gain_parts[7],
        mask_fast,
        count_fast,
        totals_one[2],
    )
    fast_skip_grad = norm_back(
        fast_final,
        fast_skip_out[1],
        fast_skip_out[2],
        gain_parts[8],
        mask_fast,
        count_fast,
        totals_one[3],
    )
    slow_expand_wg = weight_grad(stored["slow_top_low"], slow_expand_grad)
    slow_skip_wg = weight_grad(cat_low, slow_skip_grad)
    fast_expand_wg = weight_grad(stored["fast_top_low"], fast_expand_grad)
    fast_skip_wg = weight_grad(fast_low, fast_skip_grad)
    slow_spatial_top = apply_back(slow_expand_grad, slow_expand_w) * swish_slope(
        slow_spatial_out[0]
    )
    cat_grad = apply_back(slow_skip_grad, slow_skip_w)
    fast_spatial_top = apply_back(fast_expand_grad, fast_expand_w) * swish_slope(
        fast_spatial_out[0]
    )
    fast_grad = apply_back(fast_skip_grad, fast_skip_w)
    totals_two = grad_totals(
        [
            local_back(slow_spatial_top, slow_spatial_out[1]),
            local_back(fast_spatial_top, fast_spatial_out[1]),
        ]
    )
    slow_spatial_grad = norm_back(
        slow_spatial_top,
        slow_spatial_out[1],
        slow_spatial_out[2],
        gain_parts[2],
        mask_slow,
        count_slow,
        totals_two[0],
    )
    fast_spatial_grad = norm_back(
        fast_spatial_top,
        fast_spatial_out[1],
        fast_spatial_out[2],
        gain_parts[6],
        mask_fast,
        count_fast,
        totals_two[1],
    )
    slow_spatial_wg = weight_grad(pixel_taps(stored["slow_mid_pad"]), slow_spatial_grad).reshape(
        slow_spatial_w.shape
    )
    fast_spatial_wg = weight_grad(pixel_taps(stored["fast_mid_pad"]), fast_spatial_grad).reshape(
        fast_spatial_w.shape
    )
    slow_temporal_top = pixel_back(grad_rim(slow_spatial_grad), slow_spatial_w) * swish_slope(
        slow_temporal_out[0]
    )
    fast_temporal_top = pixel_back(grad_rim(fast_spatial_grad), fast_spatial_w) * swish_slope(
        fast_temporal_out[0]
    )
    totals_three = grad_totals(
        [
            local_back(slow_temporal_top, slow_temporal_out[1]),
            local_back(fast_temporal_top, fast_temporal_out[1]),
        ]
    )
    slow_temporal_grad = norm_back(
        slow_temporal_top,
        slow_temporal_out[1],
        slow_temporal_out[2],
        gain_parts[1],
        mask_slow,
        count_slow,
        totals_three[0],
    )
    fast_temporal_grad = norm_back(
        fast_temporal_top,
        fast_temporal_out[1],
        fast_temporal_out[2],
        gain_parts[5],
        mask_fast,
        count_fast,
        totals_three[1],
    )
    slow_temporal_wg = weight_grad(time_taps(cat_low), slow_temporal_grad).reshape(
        slow_temporal_w.shape
    )
    fast_temporal_wg = weight_grad(time_taps(fast_low), fast_temporal_grad).reshape(
        fast_temporal_w.shape
    )
    cat_grad = cat_grad + time_untaps(
        apply_back(slow_temporal_grad, slow_temporal_w.reshape(-1, BS)), DS + DL
    )
    fast_grad = fast_grad + time_untaps(
        apply_back(fast_temporal_grad, fast_temporal_w.reshape(-1, BF)), DF
    )
    lateral_top = cat_grad[..., DS:] * swish_slope(lateral_out[0])
    totals_four = grad_totals([local_back(lateral_top, lateral_out[1])])
    lateral_grad = norm_back(
        lateral_top,
        lateral_out[1],
        lateral_out[2],
        gain_parts[0],
        mask_slow,
        count_slow,
        totals_four[0],
    )
    lateral_wg = weight_grad(lateral_taps(fast_low), lateral_grad).reshape(lateral_w.shape)
    fast_grad = fast_grad + lateral_untaps(apply_back(lateral_grad, lateral_w.reshape(-1, DL)), DF)
    ordered = [
        totals_four[0],
        totals_three[0],
        totals_two[0],
        totals_one[0],
        totals_one[1],
        totals_three[1],
        totals_two[1],
        totals_one[2],
        totals_one[3],
    ]
    gain_grad = jnp.concatenate([member[1] for member in ordered])
    bias_grad = jnp.concatenate([member[0] for member in ordered])
    gradient_list = [
        lateral_wg,
        slow_temporal_wg,
        slow_spatial_wg,
        slow_expand_wg,
        slow_skip_wg,
        fast_temporal_wg,
        fast_spatial_wg,
        fast_expand_wg,
        fast_skip_wg,
    ]
    return (cat_grad[..., :DS], fast_grad, gradient_list, gain_grad, bias_grad)


def sum_weights(weight_grads):
    stacked = [
        jnp.stack([weight_grads[layer_index][i] for layer_index in range(LAYERS)]) for i in range(9)
    ]
    widened = tuple(
        (
            member.reshape((member.shape[0],) + (1,) * (5 - member.ndim) + member.shape[1:])
            for member in stacked
        )
    )
    partial_sums = jax.tree.map(
        lambda part: part.astype(jnp.float32),
        lax.psum_scatter(for_sending(widened), "clip", scatter_dimension=4, tiled=True),
    )
    own_sums = jax.tree.map(
        lambda part: part.astype(jnp.float32),
        lax.psum_scatter(for_sending(partial_sums), ("ha", "wa"), scatter_dimension=3, tiled=True),
    )
    results = []
    for member, summed in zip(stacked, own_sums):
        results.append(summed.reshape((summed.shape[0],) + summed.shape[1 + 5 - member.ndim :]))
    return results


def local(
    slow_in,
    fast_in,
    valid_frames,
    lateral_w,
    slow_temporal_w,
    slow_spatial_w,
    slow_expand_w,
    slow_skip_w,
    fast_temporal_w,
    fast_spatial_w,
    fast_expand_w,
    fast_skip_w,
    gains,
    biases,
    slow_cot,
    fast_cot,
):
    clips_here = slow_in.shape[0]
    local_frames = lax.dynamic_slice_in_dim(
        valid_frames, lax.axis_index("clip") * clips_here, clips_here
    )
    frame_slow = jnp.arange(ST, dtype=jnp.int32)
    frame_fast = jnp.arange(ST * ALPHA, dtype=jnp.int32)
    mask_slow = (frame_slow[None, :] < local_frames[:, None]).astype(jnp.float32)[
        :, :, None, None, None
    ]
    mask_fast = (frame_fast[None, :] < ALPHA * local_frames[:, None]).astype(jnp.float32)[
        :, :, None, None, None
    ]
    count_slow = jnp.sum(valid_frames).astype(jnp.float32) * (HT * WD)
    count_fast = count_slow * ALPHA
    all_weights = (
        lateral_w,
        slow_temporal_w,
        slow_spatial_w,
        slow_expand_w,
        slow_skip_w,
        fast_temporal_w,
        fast_spatial_w,
        fast_expand_w,
        fast_skip_w,
    )
    slow_act = slow_in
    fast_act = fast_in
    stored_list = []
    for layer_index in range(LAYERS):
        weights = [w[layer_index] for w in all_weights]
        slow_act, fast_act, stored = block_forward(
            slow_act,
            fast_act,
            weights,
            split_norms(gains[layer_index]),
            split_norms(biases[layer_index]),
            mask_slow,
            mask_fast,
            count_slow,
            count_fast,
        )
        stored_list.append(stored)
    grad_slow = slow_cot
    grad_fast = fast_cot
    weight_grads = [None] * LAYERS
    gain_grads = [None] * LAYERS
    bias_grads = [None] * LAYERS
    for layer_index in reversed(range(LAYERS)):
        weights = [w[layer_index] for w in all_weights]
        grad_slow, grad_fast, gradient_list, gain_grad, bias_grad = block_backward(
            grad_slow,
            grad_fast,
            stored_list[layer_index],
            weights,
            split_norms(gains[layer_index]),
            mask_slow,
            mask_fast,
            count_slow,
            count_fast,
        )
        weight_grads[layer_index] = gradient_list
        gain_grads[layer_index] = gain_grad
        bias_grads[layer_index] = bias_grad
    shares = sum_weights(weight_grads)
    return (
        slow_act,
        fast_act,
        grad_slow,
        grad_fast,
        shares[0],
        shares[1],
        shares[2],
        shares[3],
        shares[4],
        shares[5],
        shares[6],
        shares[7],
        shares[8],
        jnp.stack(gain_grads),
        jnp.stack(bias_grads),
    )


def solution(mesh):
    return jax.shard_map(
        local,
        mesh=mesh,
        in_specs=(
            P("clip", None, "ha", "wa", None),
            P("clip", None, "ha", "wa", None),
            P(),
            P(),
            P(),
            P(),
            P(),
            P(),
            P(),
            P(),
            P(),
            P(),
            P(),
            P(),
            P("clip", None, "ha", "wa", None),
            P("clip", None, "ha", "wa", None),
        ),
        out_specs=(
            P("clip", None, "ha", "wa", None),
            P("clip", None, "ha", "wa", None),
            P("clip", None, "ha", "wa", None),
            P("clip", None, "ha", "wa", None),
            P(None, None, ("ha", "wa"), "clip"),
            P(None, None, ("ha", "wa"), "clip"),
            P(None, None, None, ("ha", "wa"), "clip"),
            P(None, ("ha", "wa"), "clip"),
            P(None, ("ha", "wa"), "clip"),
            P(None, None, ("ha", "wa"), "clip"),
            P(None, None, None, ("ha", "wa"), "clip"),
            P(None, ("ha", "wa"), "clip"),
            P(None, ("ha", "wa"), "clip"),
            P(),
            P(),
        ),
        check_vma=False,
    )
```

profile of v0, /device:TPU:0, one launch (start us, length us, event | category | flops | bytes accessed | tf_op | source)
XLA Modules:
  0.0 1582.9 jit_solution(8524831788621900316)
XLA Ops:
  14.2 42.0 %psum.257 = f32[2,32]{1,0:T(2,128)S(1)} all-reduce(f32[2,32]{1,0:T(2,128)S(1)} %pad_maximum_fusion.86), channel_id=1, replica_groups=mesh['clip'=4,'ha'=4,'wa'=2] {'clip','ha','wa'}, use_global_device_ids=true, to_apply=%region_18.19 | all-reduce | flops 64 | bytes 512 | tf_op jit(solution)/shard_map/psum | solution.py:158
  58.3 4.2 collective-permute-start.4
  92.3 3.0 collective-permute-start.6
  102.1 41.0 %all-reduce.34 = (f32[2,32]{1,0:T(2,128)S(1)}, f32[2,256]{1,0:T(2,128)S(1)}) all-reduce(f32[2,32]{1,0:T(2,128)S(1)} %pad_maximum_fusion.87, f32[2,256]{1,0:T(2,128)S(1)} %copy-done.281), channel_id=1, replica_groups=mesh['clip'=4,'ha'=4,'wa'=2] {'clip','ha','wa'}, use_global_device_ids=true, to_apply=%region_21.22 | all-reduce | flops 576 | bytes 4608 | tf_op jit(solution)/shard_map/psum | solution.py:158
  149.5 40.3 %all-reduce.33 = (f32[2,128]{1,0:T(2,128)S(1)}, f32[2,128]{1,0:T(2,128)S(1)}, f32[2,256]{1,0:T(2,128)S(1)}) all-reduce(f32[2,128]{1,0:T(2,128)S(1)} %pad_maximum_fusion.89, f32[2,128]{1,0:T(2,128)S(1)} %pad_maximum_fusion.88, f32[2,256]{1,0:T(2,128)S(1)} %pad_maximum_fusion.71), channel_id=1, replica_groups=mesh['clip'=4,'ha'=4,'wa'=2] {'clip','ha','wa'}, use_global_device_ids=true, to_apply=%region_27.28 | all-reduce | flops 1024 | bytes 8192 | tf_op jit(solution)/shard_map/psum | solution.py:158
  196.7 4.3 collective-permute-start
  208.9 3.0 collective-permute-start.2
  212.5 4.1 copy.142
  223.7 39.8 %psum.254 = f32[2,256]{1,0:T(2,128)S(1)} all-reduce(f32[2,256]{1,0:T(2,128)S(1)} %pad_maximum_fusion.72), channel_id=1, replica_groups=mesh['clip'=4,'ha'=4,'wa'=2] {'clip','ha','wa'}, use_global_device_ids=true, to_apply=%region_9.10 | all-reduce | flops 512 | bytes 4096 | tf_op jit(solution)/shard_map/psum | solution.py:158
  265.8 40.8 %all-reduce.32 = (f32[2,256]{1,0:T(2,128)S(1)}, f32[2,1024]{1,0:T(2,128)S(1)}, f32[2,1024]{1,0:T(2,128)S(1)}) all-reduce(f32[2,256]{1,0:T(2,128)S(1)} %pad_maximum_fusion.73, f32[2,1024]{1,0:T(2,128)S(1)} %pad_maximum_fusion.67, f32[2,1024]{1,0:T(2,128)S(1)} %pad_maximum_fusion.66), channel_id=1, replica_groups=mesh['clip'=4,'ha'=4,'wa'=2] {'clip','ha','wa'}, use_global_device_ids=true, to_apply=%region_30.31 | all-reduce | flops 4608 | bytes 36864 | tf_op jit(solution)/shard_map/psum | solution.py:158
  313.2 39.6 %psum.262 = f32[2,256]{1,0:T(2,128)S(1)} all-reduce(f32[2,256]{1,0:T(2,128)S(1)} %pad_maximum_fusion.74), channel_id=1, replica_groups=mesh['clip'=4,'ha'=4,'wa'=2] {'clip','ha','wa'}, use_global_device_ids=true, to_apply=%region_33.34 | all-reduce | flops 512 | bytes 4096 | tf_op jit(solution)/shard_map/psum | solution.py:158
  357.9 4.2 collective-permute-start.8
  371.8 4.2 collective-permute-start.10
  379.2 4.0 copy.143
  389.4 41.0 %all-reduce.31 = (f32[2,256]{1,0:T(2,128)S(1)}, f32[2,32]{1,0:T(2,128)S(1)}) all-reduce(f32[2,256]{1,0:T(2,128)S(1)} %pad_maximum_fusion.75, f32[2,32]{1,0:T(2,128)S(1)} %copy-done.345), channel_id=1, replica_groups=mesh['clip'=4,'ha'=4,'wa'=2] {'clip','ha','wa'}, use_global_device_ids=true, to_apply=%region_36.37 | all-reduce | flops 576 | bytes 4608 | tf_op jit(solution)/shard_map/psum | solution.py:158
  433.2 4.2 collective-permute-start.12
  445.8 3.0 collective-permute-start.14
  452.4 3.9 concatenate.458
  458.6 41.3 %all-reduce.30 = (f32[2,1024]{1,0:T(2,128)S(1)}, f32[2,1024]{1,0:T(2,128)S(1)}, f32[2,32]{1,0:T(2,128)S(1)}) all-reduce(f32[2,1024]{1,0:T(2,128)S(1)} %pad_maximum_fusion.69, f32[2,1024]{1,0:T(2,128)S(1)} %pad_maximum_fusion.68, f32[2,32]{1,0:T(2,128)S(1)} %pad_maximum_fusion.91), channel_id=1, replica_groups=mesh['clip'=4,'ha'=4,'wa'=2] {'clip','ha','wa'}, use_global_device_ids=true, to_apply=%region_42.43 | all-reduce | flops 4160 | bytes 33280 | tf_op jit(solution)/shard_map/psum | solution.py:158
  507.6 40.4 %all-reduce.29 = (f32[2,128]{1,0:T(2,128)S(1)}, f32[2,128]{1,0:T(2,128)S(1)}, f32[2,1024]{1,0:T(2,128)S(1)}) all-reduce(f32[2,128]{1,0:T(2,128)S(1)} %pad_maximum_fusion.93, f32[2,128]{1,0:T(2,128)S(1)} %pad_maximum_fusion.92, f32[2,1024]{1,0:T(2,128)S(1)} %get-tuple-element.436), channel_id=1, replica_groups=mesh['clip'=4,'ha'=4,'wa'=2] {'clip','ha','wa'}, use_global_device_ids=true, to_apply=%region_54.55 | all-reduce | flops 2560 | bytes 20480 | tf_op jit(solution)/shard_map/psum | solution.py:158
  555.8 40.0 %all-reduce.28 = (f32[2,256]{1,0:T(2,128)S(1)}, f32[2,128]{1,0:T(2,128)S(1)}) all-reduce(f32[2,256]{1,0:T(2,128)S(1)} %pad_maximum_fusion.76, f32[2,128]{1,0:T(2,128)S(1)} %get-tuple-element.492), channel_id=1, replica_groups=mesh['clip'=4,'ha'=4,'wa'=2] {'clip','ha','wa'}, use_global_device_ids=true, to_apply=%region_62.63 | all-reduce | flops 768 | bytes 6144 | tf_op jit(solution)/shard_map/psum | solution.py:162
  597.0 4.2 collective-permute-start.16
  614.8 40.0 %all-reduce.27 = (f32[2,256]{1,0:T(2,128)}, f32[2,1024]{1,0:T(2,128)}, f32[2,32]{1,0:T(2,128)}) all-reduce(f32[2,256]{1,0:T(2,128)} %pad_maximum_fusion.77, f32[2,1024]{1,0:T(2,128)} %get-tuple-element.435, f32[2,32]{1,0:T(2,128)} %pad_maximum_fusion.94), channel_id=1, replica_groups=mesh['clip'=4,'ha'=4,'wa'=2] {'clip','ha','wa'}, use_global_device_ids=true, to_apply=%region_65.66 | all-reduce | flops 2624 | bytes 20992 | tf_op jit(solution)/shard_map/psum | solution.py:162
  667.6 4.2 collective-permute-start.24
  674.3 3.7 collective-permute-done.25
  685.2 3.8 concatenate.480
  692.2 40.5 %all-reduce.26 = (f32[2,1024]{1,0:T(2,128)}, f32[2,256]{1,0:T(2,128)}, f32[2,32]{1,0:T(2,128)}, f32[2,128]{1,0:T(2,128)}) all-reduce(f32[2,1024]{1,0:T(2,128)} %get-tuple-element.434, f32[2,256]{1,0:T(2,128)} %pad_maximum_fusion.80, f32[2,32]{1,0:T(2,128)} %pad_maximum_fusion.95, ...), channel_id=1, replica_groups=mesh['clip'=4,'ha'=4,'wa'=2] {'clip','ha','wa'}, use_global_device_ids=true, to_apply=%region_70.71 | all-reduce | flops 2880 | bytes 23040 | tf_op jit(solution)/shard_map/psum | solution.py:162
  755.8 3.2 fusion.121
  759.6 41.2 %all-reduce.25 = (f32[2,256]{1,0:T(2,128)S(1)}, f32[2,128]{1,0:T(2,128)S(1)}) all-reduce(f32[2,256]{1,0:T(2,128)} %pad_maximum_fusion.78, f32[2,128]{1,0:T(2,128)S(1)} %get-tuple-element.490), channel_id=1, replica_groups=mesh['clip'=4,'ha'=4,'wa'=2] {'clip','ha','wa'}, use_global_device_ids=true, to_apply=%region_73.74 | all-reduce | flops 768 | bytes 6144 | tf_op jit(solution)/shard_map/psum | solution.py:162
  802.1 4.2 collective-permute-start.20
  819.4 41.0 %all-reduce.24 = (f32[2,256]{1,0:T(2,128)S(1)}, f32[2,1024]{1,0:T(2,128)S(1)}, f32[2,32]{1,0:T(2,128)S(1)}) all-reduce(f32[2,256]{1,0:T(2,128)S(1)} %pad_maximum_fusion.79, f32[2,1024]{1,0:T(2,128)S(1)} %copy-done.203, f32[2,32]{1,0:T(2,128)S(1)} %pad_maximum_fusion.96), channel_id=1, replica_groups=mesh['clip'=4,'ha'=4,'wa'=2] {'clip','ha','wa'}, use_global_device_ids=true, to_apply=%region_76.77 | all-reduce | flops 2624 | bytes 20992 | tf_op jit(solution)/shard_map/psum | solution.py:162
  862.0 4.2 collective-permute-start.28
  882.3 3.9 concatenate.488
  888.7 40.8 %all-reduce.23 = (f32[2,256]{1,0:T(2,128)}, f32[2,32]{1,0:T(2,128)S(1)}, f32[2,128]{1,0:T(2,128)}) all-reduce(f32[2,256]{1,0:T(2,128)S(1)} %pad_maximum_fusion.81, f32[2,32]{1,0:T(2,128)S(1)} %pad_maximum_fusion.97, f32[2,128]{1,0:T(2,128)S(1)} %copy-done.346), channel_id=1, replica_groups=mesh['clip'=4,'ha'=4,'wa'=2] {'clip','ha','wa'}, use_global_device_ids=true, to_apply=%region_109.110 | all-reduce | flops 832 | bytes 6656 | tf_op jit(solution)/shard_map/psum | solution.py:162
  952.2 6.9 copy.147
  971.1 10.7 copy.144
  985.1 3.0 copy.140
  1001.6 3.8 concatenate.534
  1028.7 216.4 %all-reduce.43.cloned.1.call-done = (bf16[2,1,5,128,256]{3,0,2,1,4:T(2,128)(2,1)}, bf16[2,3,3,256,256]{3,0,2,1,4:T(2,128)(2,1)}, bf16[2,1,3,1280,256]{3,0,2,1,4:T(2,128)(2,1)}) async-done(((bf16[2,1,5,128,256]{3,0,2,1,4:T(2,128)(2,1)}, bf16[2,3,3,256,256]{3,0,2,1,4:T(2,128)(2,1)}, bf16[2,1,3,1280,256]{3,0,2,1,4:T(2,128)(2,1)}), (bf16[2,1,5,128,256]{3,0,2,1,4:T(2,128)(2,1)}, ...) | async-done | bytes 6946832
  1248.8 3.1 copy.148
  1254.4 80.7 %copy.212 = bf16[2,1,3,1280,64]{0,2,1,4,3:T(4,128)(2,1)} copy(bf16[2,1,3,1280,64]{3,0,2,1,4:T(2,128)(2,1)S(1)} %constant_dynamic-slice_fusion.3) | data formatting | bytes 1966080
  1335.1 124.5 %reshape.2353 = bf16[1280,384]{1,0:T(8,128)(2,1)} reshape(bf16[1280,64,1,3,2]{4,3,2,1,0:T(4,128)(2,1)} %bitcast.494) | data formatting | bytes 1966080
  1460.0 18.6 %all-reduce.19 = bf16[2,3,3,32,32]{3,0,2,1,4:T(2,128)(2,1)S(1)} all-reduce(bf16[2,3,3,32,32]{3,0,2,1,4:T(2,128)(2,1)S(1)} %copy.157), channel_id=14, replica_groups=mesh['clip'=4,'ha'=4,'wa'=2] {'clip'}, use_global_device_ids=true, to_apply=%region_127.128.clone | all-reduce | flops 18432 | bytes 73728
  1491.6 25.6 %all-reduce.35 = (bf16[2,3,3,32,8]{4,3,2,1,0:T(8,128)(2,1)S(1)}, bf16[2,1,1,32,32]{4,3,2,1,0:T(8,128)(2,1)S(1)}, bf16[2,1,1,128,32]{4,0,2,1,3:T(2,128)(2,1)S(1)}) all-reduce(bf16[2,3,3,32,8]{4,3,2,1,0:T(8,128)(2,1)} %copy.158, ...), channel_id=15, replica_groups=mesh['clip'=4,'ha'=4,'wa'=2] {'ha','wa'}, use_global_device_ids=true, to_apply=%region_128.129.clone | all-reduce | flops 14848 | bytes 59392
  1523.7 10.0 reduce-scatter.30.cloned.1.call-done
  1533.7 14.1 reshape.2354
  1547.8 14.4 copy.213
  1563.2 11.1 reduce-scatter.26.cloned.1.call-done
  (1232 shorter events, 332.1 us)
Async XLA Ops:
  7.2 1007.7 %reduce-scatter.32.cloned.1.call-start = ((), (), s32[]{:S(2)}) async-start(), calls=%async_computation.15 | async-start | bytes 61440
  58.3 32.6 %collective-permute-start.4 = (bf16[1,32,1,8,32]{4,3,2,1,0:T(8,128)(2,1)}, bf16[1,32,1,8,32]{4,3,2,1,0:T(8,128)(2,1)S(1)}, u32[]{:S(2)}, u32[]{:S(2)}) collective-permute-start(bf16[1,32,1,8,32]{4,3,2,1,0:T(8,128)(2,1)} %get-tuple-element.333), channel_id=1, source_target_pairs={{0,2},{2,4},{4,6},{1,3},{3,5},{5,7},{8,10},{10,12},{12,14},{9,11},... | collective-permute-start | bytes 49160 | tf_op jit(solution)/shard_map/ppermute | solution.py:28
  62.5 28.4 %collective-permute-start.5 = (bf16[1,32,1,8,32]{4,3,2,1,0:T(8,128)(2,1)}, bf16[1,32,1,8,32]{4,3,2,1,0:T(8,128)(2,1)S(1)}, u32[]{:S(2)}, u32[]{:S(2)}) collective-permute-start(bf16[1,32,1,8,32]{4,3,2,1,0:T(8,128)(2,1)} %get-tuple-element.334), channel_id=1, source_target_pairs={{2,0},{4,2},{6,4},{3,1},{5,3},{7,5},{10,8},{12,10},{14,12},{11,9},... | collective-permute-start | bytes 49160 | tf_op jit(solution)/shard_map/ppermute | solution.py:29
  72.5 120.2 %copy-start.8 = (f32[32,4,8,128]{3,2,1,0:T(8,128)}, f32[32,4,8,128]{3,2,1,0:T(8,128)S(1)}, u32[]{:S(2)}) copy-start(f32[32,4,8,128]{3,2,1,0:T(8,128)S(1)} %fusion.171) | copy-start | bytes 1572868
  78.8 65.1 %copy-start.16 = (f32[8,4,8,256]{3,2,1,0:T(8,128)}, f32[8,4,8,256]{3,2,1,0:T(8,128)S(1)}, u32[]{:S(2)}) copy-start(f32[8,4,8,256]{3,2,1,0:T(8,128)S(1)} %get-tuple-element.495) | copy-start | bytes 786436
  84.4 119.7 %copy-start.18 = (bf16[1,8,4,8,1024]{4,3,2,1,0:T(8,128)(2,1)}, bf16[1,8,4,8,1024]{4,3,2,1,0:T(8,128)(2,1)S(1)}, u32[]{:S(2)}) copy-start(bf16[1,8,4,8,1024]{4,3,2,1,0:T(8,128)(2,1)S(1)} %convert_element_type.273) | copy-start | bytes 1572868
  91.0 4.5 collective-permute-start.7
  92.3 4.0 collective-permute-start.6
  149.5 72.7 %copy-start.34 = (f32[8,4,8,256]{3,2,1,0:T(8,128)}, f32[8,4,8,256]{3,2,1,0:T(8,128)S(1)}, u32[]{:S(2)}) copy-start(f32[8,4,8,256]{3,2,1,0:T(8,128)S(1)} %get-tuple-element.497) | copy-start | bytes 786436
  196.7 9.2 collective-permute-start
  201.1 5.8 collective-permute-start.1
  207.6 12.1 collective-permute-start.3
  208.9 10.8 collective-permute-start.2
  313.2 74.1 %copy-start.36 = (f32[8,4,8,256]{3,2,1,0:T(8,128)}, f32[8,4,8,256]{3,2,1,0:T(8,128)S(1)}, u32[]{:S(2)}) copy-start(f32[8,4,8,256]{3,2,1,0:T(8,128)S(1)} %get-tuple-element.500) | copy-start | bytes 786436
  357.9 11.9 collective-permute-start.8
  362.1 7.7 collective-permute-start.9
  370.5 12.6 collective-permute-start.11
  371.8 11.4 collective-permute-start.10
  433.2 11.1 collective-permute-start.12
  437.4 7.0 collective-permute-start.13
  444.5 5.2 collective-permute-start.15
  445.8 4.0 collective-permute-start.14
  597.0 8.9 collective-permute-start.16
  601.1 5.8 collective-permute-start.17
  607.0 3.2 collective-permute-start.19
  608.3 3.1 collective-permute-start.18
  667.6 6.7 collective-permute-start.24
  671.8 6.2 collective-permute-start.25
  678.1 3.5 collective-permute-start.27
  679.4 3.2 collective-permute-start.26
  802.1 9.9 collective-permute-start.20
  806.3 5.8 collective-permute-start.21
  812.2 2.6 collective-permute-start.23
  813.5 3.1 collective-permute-start.22
  862.0 13.1 collective-permute-start.28
  866.2 8.9 collective-permute-start.29
  875.3 3.5 collective-permute-start.31
  876.6 3.2 collective-permute-start.30
  932.3 92.1 %reduce-scatter.20.cloned.1.call-start = ((), (), s32[]{:S(2)}) async-start(), calls=%async_computation.9 | async-start | bytes 1310720 | tf_op jit(solution)/shard_map/reduce_scatter | solution.py:491
  934.7 92.0 %reduce-scatter.36.cloned.1.call-start = ((), (), s32[]{:S(2)}) async-start(), calls=%async_computation.17 | async-start | bytes 40960
  966.4 278.7 %all-reduce.43.cloned.1.call-start = ((), (), s32[]{:S(2)}) async-start(), calls=%async_computation.19 | async-start | bytes 13893632
  988.1 499.4 %reduce-scatter.24.cloned.1.call-start = ((), (), s32[]{:S(2)}) async-start(), calls=%async_computation.11 | async-start | bytes 6553600 | tf_op jit(solution)/shard_map/reduce_scatter | solution.py:491
  994.2 495.1 %reduce-scatter.34.cloned.1.call-start = ((), (), s32[]{:S(2)}) async-start(), calls=%async_computation.16 | async-start | bytes 36864
  1018.1 472.7 %reduce-scatter.28.cloned.1.call-start = ((), (), s32[]{:S(2)}) async-start(), calls=%async_computation.13 | async-start | bytes 81920 | tf_op jit(solution)/shard_map/reduce_scatter | solution.py:491
  1019.6 499.5 %reduce-scatter.22.cloned.1.call-start = ((), (), s32[]{:S(2)}) async-start(), calls=%async_computation.10 | async-start | bytes 294912 | tf_op jit(solution)/shard_map/reduce_scatter | solution.py:495
  1024.5 495.9 %all-reduce.41.cloned.1.call-start = ((), (), s32[]{:S(2)}) async-start(), calls=%async_computation.18 | async-start | bytes 3014656
  1251.9 281.8 %reduce-scatter.30.cloned.1.call-start = ((), (), s32[]{:S(2)}) async-start(), calls=%async_computation.14 | async-start | bytes 1105920
  1459.8 114.5 %reduce-scatter.26.cloned.1.call-start = ((), (), s32[]{:S(2)}) async-start(), calls=%async_computation.12 | async-start | bytes 1474560 | tf_op jit(solution)/shard_map/reduce_scatter | solution.py:495
  (371 other events, 3334.4 us)
Sparse Core Ops, SparseCore 0:
  932.5 19.4 reduce-scatter.31
  954.4 25.3 reduce-scatter.19
  982.0 17.6 reduce-scatter.35
  1002.3 242.8 all-reduce.42
  1247.4 92.5 reduce-scatter.23
  1343.7 31.7 reduce-scatter.33
  1378.3 19.0 reduce-scatter.27
  1400.7 31.7 reduce-scatter.21
  1436.4 58.7 all-reduce.40
  1498.6 35.0 reduce-scatter.29
  1537.0 37.2 reduce-scatter.25
where the time goes:
time: 1600 us; the launch traced here: 1580 us
  blocking collectives  654 us (41%)
  local copies, waits for them, and re-layouts  393 us (25%)
  waiting for transfers between devices  249 us (16%)
  other arithmetic  118 us (7%)
  starting transfers between devices  73.8 us (5%)
  matrix products  69.3 us (4%)
  between operations  24.6 us (2%)
    psum x9, blocking collectives, moment_totals(): return [lax.psum(one_term, ('clip', 'ha', 'wa')) for one_term in term_list]  366 us
    unnamed x820, local copies, waits for them, and re-layouts  282 us
    psum x6, blocking collectives, grad_totals(): return [lax.psum(one_term, ('clip', 'ha', 'wa')) for one_term in term_list]  244 us
    unnamed x17, waiting for transfers between devices  227 us
    ppermute x16, starting transfers between devices, with_halo(): before = lax.ppermute(last, axis, up)  52.1 us
    unnamed x2, blocking collectives  44.2 us
  transfers between devices with their start and end apart: 43, of which 12 were waited for; matrix products, arithmetic and copies ran while one was open for 27% of the time, Pallas kernels for 0%

commit v1 on v0

--- a/solution.py
+++ b/solution.py
@@ -154,12 +154,26 @@
     )
 
 
+ALL_AXES = ("clip", "ha", "wa")
+
+
 def moment_totals(term_list):
-    return [lax.psum(one_term, ("clip", "ha", "wa")) for one_term in term_list]
-
-
-def grad_totals(term_list):
-    return [lax.psum(one_term, ("clip", "ha", "wa")) for one_term in term_list]
+    flat = jnp.concatenate([one_term.reshape(-1) for one_term in term_list])
+    length = flat.shape[0]
+    padded = -(-length // 1024) * 1024
+    rows = jnp.pad(flat, (0, padded - length)).reshape(8, padded // 8)
+    count = lax.axis_size(ALL_AXES)
+    sent = jnp.broadcast_to(rows[None], (count,) + rows.shape)
+    total = jnp.sum(lax.all_to_all(sent, ALL_AXES, 0, 0), axis=0).reshape(-1)
+    results = []
+    offset = 0
+    for one_term in term_list:
+        results.append(total[offset : offset + one_term.size].reshape(one_term.shape))
+        offset += one_term.size
+    return results
+
+
+grad_totals = moment_totals
 
 
 def normalize(values, totals, count_all, gain_part, bias_part):
@@ -476,28 +490,51 @@
     return (cat_grad[..., :DS], fast_grad, gradient_list, gain_grad, bias_grad)
 
 
+def scatter_sum(blocks):
+    for axis, dim in (("wa", 2), ("ha", 1), ("clip", 0)):
+        place = lax.axis_index(axis)
+        count = lax.axis_size(axis)
+        step = 1
+        while step < count:
+            step *= 2
+        step //= 2
+        while step >= 1:
+            half = blocks.shape[dim] // 2
+            bit = (place // step) % 2
+            kept = lax.dynamic_slice_in_dim(blocks, bit * half, half, dim)
+            sent = lax.dynamic_slice_in_dim(blocks, (1 - bit) * half, half, dim)
+            got = lax.ppermute(sent, axis, [(i, i ^ step) for i in range(count)])
+            blocks = (kept.astype(jnp.float32) + got.astype(jnp.float32)).astype(jnp.bfloat16)
+            step //= 2
+    return blocks
+
+
 def sum_weights(weight_grads):
-    stacked = [
-        jnp.stack([weight_grads[layer_index][i] for layer_index in range(LAYERS)]) for i in range(9)
-    ]
-    widened = tuple(
-        (
-            member.reshape((member.shape[0],) + (1,) * (5 - member.ndim) + member.shape[1:])
-            for member in stacked
-        )
-    )
-    partial_sums = jax.tree.map(
-        lambda part: part.astype(jnp.float32),
-        lax.psum_scatter(for_sending(widened), "clip", scatter_dimension=4, tiled=True),
-    )
-    own_sums = jax.tree.map(
-        lambda part: part.astype(jnp.float32),
-        lax.psum_scatter(for_sending(partial_sums), ("ha", "wa"), scatter_dimension=3, tiled=True),
-    )
-    results = []
-    for member, summed in zip(stacked, own_sums):
-        results.append(summed.reshape((summed.shape[0],) + summed.shape[1 + 5 - member.ndim :]))
-    return results
+    clips = lax.axis_size("clip")
+    tiles = lax.axis_size(("ha", "wa"))
+    per_layer = []
+    for layer_grads in weight_grads:
+        pieces = []
+        shapes = []
+        for member in layer_grads:
+            rows, columns = member.shape[-2:]
+            low = member.astype(jnp.bfloat16).reshape(-1, tiles, rows // tiles, clips, columns // clips)
+            pieces.append(jnp.transpose(low, (3, 1, 0, 2, 4)).reshape(clips * tiles, -1))
+            shapes.append(member.shape[:-2] + (rows // tiles, columns // clips))
+        flat = jnp.concatenate(pieces, axis=1)
+        length = -(-flat.shape[1] // 2048) * 2048
+        flat = jnp.pad(flat, ((0, 0), (0, length - flat.shape[1])))
+        summed = scatter_sum(flat.reshape(clips, -1, lax.axis_size("wa"), length // 128, 128)).reshape(-1)
+        offset = 0
+        shares = []
+        for shape in shapes:
+            size = 1
+            for d in shape:
+                size *= d
+            shares.append(summed[offset : offset + size].reshape(shape).astype(jnp.float32))
+            offset += size
+        per_layer.append(shares)
+    return [jnp.stack(group) for group in zip(*per_layer)]
 
 
 def local(

time: 1600 us -> 767 us (0.48)
  blocking collectives: 654 us -> 0 us
  local copies, waits for them, and re-layouts: 393 us -> 264 us
  waiting for transfers between devices: 249 us -> 139 us
  starting transfers between devices: 73.8 us -> 162 us
    psum x15 -> x0, blocking collectives: 610 us -> none  [the longest x9 366 us: moment_totals(): return [lax.psum(one_term, ('clip', 'ha', 'wa')) for one_term in term_list]]
    unnamed x17 -> x0, waiting for transfers between devices: 227 us -> none
    unnamed x820 -> x846, local copies, waits for them, and re-layouts: 282 us -> 74.7 us
    all_to_all x0 -> x16, starting transfers between devices: none -> 80.1 us  [moment_totals(): total = jnp.sum(lax.all_to_all(sent, ALL_AXES, 0, 0), axis=0).reshape(-1)]
    ppermute x0 -> x10, waiting for transfers between devices: none -> 78.8 us  [scatter_sum(): got = lax.ppermute(sent, axis, [(i, i ^ step) for i in range(count)])]
    reshape x0 -> x57, local copies, waits for them, and re-layouts: none -> 60.5 us  [the longest x31 32.3 us: sum_weights(): member.astype(jnp.bfloat16)]
    unnamed x2 -> x0, blocking collectives: 44.2 us -> none
    all_to_all x0 -> x16, waiting for transfers between devices: none -> 33.4 us  [moment_totals(): total = jnp.sum(lax.all_to_all(sent, ALL_AXES, 0, 0), axis=0).reshape(-1)]
  transfers between devices with their start and end apart: 43 -> 58, of which waited for: 12 -> 27; matrix products, arithmetic and copies ran while one was open for 27% -> 37% of each run, Pallas kernels for 0% -> 0%
where the time goes in v1:
time: 767 us; the launch traced here: 753 us
  local copies, waits for them, and re-layouts  264 us (34%)
  starting transfers between devices  162 us (21%)
  waiting for transfers between devices  139 us (18%)
  other arithmetic  116 us (15%)
  matrix products  62.6 us (8%)
  between operations  8.78 us (1%)
    all_to_all x16, starting transfers between devices, moment_totals(): total = jnp.sum(lax.all_to_all(sent, ALL_AXES, 0, 0), axis=0).reshape(-1)  80.1 us
    ppermute x10, waiting for transfers between devices, scatter_sum(): got = lax.ppermute(sent, axis, [(i, i ^ step) for i in range(count)])  78.8 us
    unnamed x846, local copies, waits for them, and re-layouts  74.7 us
    ppermute x16, starting transfers between devices, with_halo(): before = lax.ppermute(last, axis, up)  49.2 us
    all_to_all x16, waiting for transfers between devices, moment_totals(): total = jnp.sum(lax.all_to_all(sent, ALL_AXES, 0, 0), axis=0).reshape(-1)  33.4 us
    reshape x31, local copies, waits for them, and re-layouts, sum_weights(): member.astype(jnp.bfloat16)  32.3 us
    dot_general x22, matrix products, apply_weight(): jnp.einsum('...k,kn->...n', inputs, weight, preferred_element_type=jnp.fl...  28.6 us
    reshape x14, local copies, waits for them, and re-layouts, sum_weights(): jnp.transpose(low, (3, 1, 0, 2, 4)).reshape(clips * tiles, -1)  26.2 us
  transfers between devices with their start and end apart: 58, of which 27 were waited for; matrix products, arithmetic and copies ran while one was open for 37% of the time, Pallas kernels for 0%

profile of v1, /device:TPU:0, one launch (start us, length us, event | category | flops | bytes accessed | tf_op | source)
XLA Modules:
  0.0 752.7 jit_solution(7000399406939190659)
XLA Ops:
  8.2 7.3 all-to-all-start
  22.5 4.5 fusion.258
  67.1 6.8 all-to-all-start.1
  83.1 4.0 all-to-all-done.1
  116.9 4.1 all-to-all-done.2
  130.6 6.6 all-to-all-done.4
  150.1 4.0 collective-permute-done.9
  162.1 3.8 concatenate.442
  177.8 5.8 all-to-all-start.5
  208.8 3.9 collective-permute-done.13
  223.4 5.5 all-to-all-start.6
  231.7 4.0 copy.142
  243.3 5.1 all-to-all-start.7
  253.3 5.7 all-to-all-done.7
  286.0 4.6 all-to-all-done.8
  313.0 4.3 reshape.2479
  321.9 3.8 collective-permute-start.16
  327.2 4.5 collective-permute-start.20
  334.5 3.8 collective-permute-done.21
  356.2 6.4 all-to-all-start.10
  365.9 4.0 reshape.2476
  385.2 4.0 copy.143
  389.2 5.4 reshape.2472
  394.6 4.4 copy.144
  399.0 4.8 reshape.2473
  405.8 5.5 all-to-all-start.11
  413.6 6.0 all-to-all-done.11
  476.7 6.1 all-to-all-start.13
  489.7 4.3 reshape.2453
  498.6 3.8 collective-permute-start.24
  504.0 4.5 collective-permute-start.28
  511.3 3.8 collective-permute-done.29
  532.9 6.4 all-to-all-start.14
  542.8 4.0 reshape.2450
  556.4 5.3 all-to-all-start.15
  564.2 4.1 copy.125
  570.1 5.4 reshape.2446
  575.5 4.5 copy.126
  580.0 4.9 reshape.2447
  608.5 3.9 add_convert_fusion
  628.4 4.1 add_convert_fusion.1
  638.5 15.6 %collective-permute-done.38 = bf16[4,2,1,832,128]{4,3,2,1,0:T(8,128)(2,1)} collective-permute-done((bf16[4,2,1,832,128]{4,3,2,1,0:T(8,128)(2,1)}, bf16[4,2,1,832,128]{4,3,2,1,0:T(8,128)(2,1)}, u32[]{:S(2)}, u32[]{:S(2)}) %collective-permute-start.38) | collective-permute-done | bytes 1703968 | tf_op jit(solution)/shard_map/ppermute | solution.py:506
  667.6 10.8 %collective-permute-done.39 = bf16[4,1,1,832,128]{4,3,2,1,0:T(8,128)(2,1)} collective-permute-done((bf16[4,1,1,832,128]{4,3,2,1,0:T(8,128)(2,1)}, bf16[4,1,1,832,128]{4,3,2,1,0:T(8,128)(2,1)}, u32[]{:S(2)}, u32[]{:S(2)}) %collective-permute-start.39) | collective-permute-done | bytes 852000 | tf_op jit(solution)/shard_map/ppermute | solution.py:506
  679.8 10.3 %collective-permute-done.33 = bf16[4,2,1,832,128]{4,3,2,1,0:T(8,128)(2,1)} collective-permute-done((bf16[4,2,1,832,128]{4,3,2,1,0:T(8,128)(2,1)}, bf16[4,2,1,832,128]{4,3,2,1,0:T(8,128)(2,1)}, u32[]{:S(2)}, u32[]{:S(2)}) %collective-permute-start.33) | collective-permute-done | bytes 1703968 | tf_op jit(solution)/shard_map/ppermute | solution.py:506
  696.9 18.0 %collective-permute-done.40 = bf16[2,1,1,832,128]{4,3,2,1,0:T(8,128)(2,1)S(1)} collective-permute-done((bf16[2,1,1,832,128]{4,3,2,1,0:T(8,128)(2,1)S(1)}, bf16[2,1,1,832,128]{4,3,2,1,0:T(8,128)(2,1)S(1)}, u32[]{:S(2)}, u32[]{:S(2)}) %collective-permute-start.40) | collective-permute-done | bytes 426016 | tf_op jit(solution)/shard_map/ppermute | solution.py:506
  719.3 6.0 collective-permute-done.41
  726.4 11.8 %collective-permute-done.35 = bf16[2,1,1,832,128]{4,3,2,1,0:T(8,128)(2,1)S(1)} collective-permute-done((bf16[2,1,1,832,128]{4,3,2,1,0:T(8,128)(2,1)S(1)}, bf16[2,1,1,832,128]{4,3,2,1,0:T(8,128)(2,1)S(1)}, u32[]{:S(2)}, u32[]{:S(2)}) %collective-permute-start.35) | collective-permute-done | bytes 426016 | tf_op jit(solution)/shard_map/ppermute | solution.py:506
  738.5 6.3 collective-permute-done.36
  (1400 shorter events, 467.1 us)
Async XLA Ops:
  8.2 33.3 %all-to-all-start = ((f32[32,8,128]{2,1,0:T(8,128)}), f32[32,8,128]{2,1,0:T(8,128)S(1)}, u32[]{:S(2)}, u32[]{:S(2)}) async-start(f32[32,8,128]{2,1,0:T(8,128)} %broadcast_in_dim.65), calls=%async_computation | async-start | bytes 262144 | tf_op jit(solution)/shard_map/all_to_all | solution.py:167
  43.0 10.8 %collective-permute-start = (bf16[1,32,1,8,32]{4,3,2,1,0:T(8,128)(2,1)S(1)}, bf16[1,32,1,8,32]{4,3,2,1,0:T(8,128)(2,1)S(1)}, u32[]{:S(2)}, u32[]{:S(2)}) collective-permute-start(bf16[1,32,1,8,32]{4,3,2,1,0:T(8,128)(2,1)S(1)} %get-tuple-element.274), channel_id=1, source_target_pairs={{0,2},{2,4},{4,6},{1,3},{3,5},{5,7},{8,10},{10,12},{12,14},{9,11},... | collective-permute-start | bytes 49160 | tf_op jit(solution)/shard_map/ppermute | solution.py:28
  46.7 7.1 collective-permute-start.1
  54.0 5.2 collective-permute-start.3
  55.3 4.0 collective-permute-start.2
  67.1 20.0 %all-to-all-start.1 = ((f32[32,8,384]{2,1,0:T(8,128)}), f32[32,8,384]{2,1,0:T(8,128)}, u32[]{:S(2)}, u32[]{:S(2)}) async-start(f32[32,8,384]{2,1,0:T(8,128)} %broadcast_in_dim.67), calls=%async_computation.1 | async-start | bytes 786432 | tf_op jit(solution)/shard_map/all_to_all | solution.py:167
  90.2 4.9 collective-permute-start.4
  92.6 5.8 collective-permute-start.5
  98.5 4.6 collective-permute-start.7
  109.0 12.0 %all-to-all-start.2 = ((f32[32,8,128]{2,1,0:T(8,128)}), f32[32,8,128]{2,1,0:T(8,128)S(1)}, u32[]{:S(2)}, u32[]{:S(2)}) async-start(f32[32,8,128]{2,1,0:T(8,128)} %broadcast_in_dim.69), calls=%async_computation.2 | async-start | bytes 262144 | tf_op jit(solution)/shard_map/all_to_all | solution.py:167
  126.5 10.8 %all-to-all-start.4 = ((f32[32,8,128]{2,1,0:T(8,128)}), f32[32,8,128]{2,1,0:T(8,128)S(1)}, u32[]{:S(2)}, u32[]{:S(2)}) async-start(f32[32,8,128]{2,1,0:T(8,128)} %broadcast_in_dim.73), calls=%async_computation.4 | async-start | bytes 262144 | tf_op jit(solution)/shard_map/all_to_all | solution.py:167
  138.0 30.4 %all-to-all-start.3 = ((f32[32,8,256]{2,1,0:T(8,128)}), f32[32,8,256]{2,1,0:T(8,128)}, u32[]{:S(2)}, u32[]{:S(2)}) async-start(f32[32,8,256]{2,1,0:T(8,128)} %broadcast_in_dim.71), calls=%async_computation.3 | async-start | bytes 524288 | tf_op jit(solution)/shard_map/all_to_all | solution.py:167
  144.5 5.6 collective-permute-start.8
  148.0 6.2 collective-permute-start.9
  154.3 5.2 collective-permute-start.11
  155.6 4.0 collective-permute-start.10
  177.8 22.4 %all-to-all-start.5 = ((f32[32,8,384]{2,1,0:T(8,128)}), f32[32,8,384]{2,1,0:T(8,128)}, u32[]{:S(2)}, u32[]{:S(2)}) async-start(f32[32,8,384]{2,1,0:T(8,128)} %broadcast_in_dim.75), calls=%async_computation.5 | async-start | bytes 786432 | tf_op jit(solution)/shard_map/all_to_all | solution.py:167
  203.3 5.5 collective-permute-start.12
  207.0 5.8 collective-permute-start.13
  212.8 4.8 collective-permute-start.15
  223.4 13.8 %all-to-all-start.6 = ((f32[32,8,128]{2,1,0:T(8,128)}), f32[32,8,128]{2,1,0:T(8,128)S(1)}, u32[]{:S(2)}, u32[]{:S(2)}) async-start(f32[32,8,128]{2,1,0:T(8,128)} %broadcast_in_dim.77), calls=%async_computation.6 | async-start | bytes 262144 | tf_op jit(solution)/shard_map/all_to_all | solution.py:167
  243.3 15.7 %all-to-all-start.7 = ((f32[32,8,256]{2,1,0:T(8,128)}), f32[32,8,256]{2,1,0:T(8,128)}, u32[]{:S(2)}, u32[]{:S(2)}) async-start(f32[32,8,256]{2,1,0:T(8,128)} %broadcast_in_dim.79), calls=%async_computation.7 | async-start | bytes 524288 | tf_op jit(solution)/shard_map/all_to_all | solution.py:167
  269.4 21.2 %all-to-all-start.8 = ((f32[32,8,640]{2,1,0:T(8,128)}), f32[32,8,640]{2,1,0:T(8,128)}, u32[]{:S(2)}, u32[]{:S(2)}) async-start(f32[32,8,640]{2,1,0:T(8,128)} %broadcast_in_dim.81), calls=%async_computation.8 | async-start | bytes 1310720 | tf_op jit(solution)/shard_map/all_to_all | solution.py:167
  303.1 17.9 %all-to-all-start.9 = ((f32[32,8,128]{2,1,0:T(8,128)}), f32[32,8,128]{2,1,0:T(8,128)S(1)}, u32[]{:S(2)}, u32[]{:S(2)}) async-start(f32[32,8,128]{2,1,0:T(8,128)} %broadcast_in_dim.83), calls=%async_computation.9 | async-start | bytes 262144 | tf_op jit(solution)/shard_map/all_to_all | solution.py:167
  321.9 26.5 %collective-permute-start.16 = (bf16[1,8,1,8,256]{4,3,2,1,0:T(8,128)(2,1)}, bf16[1,8,1,8,256]{4,3,2,1,0:T(8,128)(2,1)S(1)}, u32[]{:S(2)}, u32[]{:S(2)}) collective-permute-start(bf16[1,8,1,8,256]{4,3,2,1,0:T(8,128)(2,1)} %get-tuple-element.300), channel_id=1, source_target_pairs={{0,2},{2,4},{4,6},{1,3},{3,5},{5,7},{8,10},{10,12},{12,14},{9,11},... | collective-permute-start | bytes 98312 | tf_op jit(solution)/shard_map/ppermute | solution.py:28
  325.7 22.8 %collective-permute-start.17 = (bf16[1,8,1,8,256]{4,3,2,1,0:T(8,128)(2,1)S(1)}, bf16[1,8,1,8,256]{4,3,2,1,0:T(8,128)(2,1)S(1)}, u32[]{:S(2)}, u32[]{:S(2)}) collective-permute-start(bf16[1,8,1,8,256]{4,3,2,1,0:T(8,128)(2,1)S(1)} %get-tuple-element.301), channel_id=1, source_target_pairs={{2,0},{4,2},{6,4},{3,1},{5,3},{7,5},{10,8},{12,10},{14,12},{11,9},... | collective-permute-start | bytes 98312 | tf_op jit(solution)/shard_map/ppermute | solution.py:29
  327.2 7.3 collective-permute-start.20
  331.8 6.5 collective-permute-start.21
  356.2 14.6 %all-to-all-start.10 = ((f32[32,8,128]{2,1,0:T(8,128)}), f32[32,8,128]{2,1,0:T(8,128)}, u32[]{:S(2)}, u32[]{:S(2)}) async-start(f32[32,8,128]{2,1,0:T(8,128)} %broadcast_in_dim.85), calls=%async_computation.10 | async-start | bytes 262144 | tf_op jit(solution)/shard_map/all_to_all | solution.py:167
  405.8 13.8 %all-to-all-start.11 = ((f32[32,8,128]{2,1,0:T(8,128)}), f32[32,8,128]{2,1,0:T(8,128)S(1)}, u32[]{:S(2)}, u32[]{:S(2)}) async-start(f32[32,8,128]{2,1,0:T(8,128)} %broadcast_in_dim.87), calls=%async_computation.11 | async-start | bytes 262144 | tf_op jit(solution)/shard_map/all_to_all | solution.py:167
  443.8 24.0 %all-to-all-start.12 = ((f32[32,8,640]{2,1,0:T(8,128)}), f32[32,8,640]{2,1,0:T(8,128)}, u32[]{:S(2)}, u32[]{:S(2)}) async-start(f32[32,8,640]{2,1,0:T(8,128)} %broadcast_in_dim.89), calls=%async_computation.12 | async-start | bytes 1310720 | tf_op jit(solution)/shard_map/all_to_all | solution.py:167
  467.8 140.7 %collective-permute-start.37 = (bf16[4,4,1,832,128]{4,3,2,1,0:T(8,128)(2,1)}, bf16[4,4,1,832,128]{4,3,2,1,0:T(8,128)(2,1)}, u32[]{:S(2)}, u32[]{:S(2)}) collective-permute-start(bf16[4,4,1,832,128]{4,3,2,1,0:T(8,128)(2,1)} %constant_dynamic-slice_fusion.4), channel_id=1, source_target_pairs={{0,1},{1,0},{2,3},{3,2},{4,5},{5,4},{6,7},{7,6},{8,9},{9,8},{10,11... | collective-permute-start | bytes 10223624 | tf_op jit(solution)/shard_map/ppermute | solution.py:506
  476.7 21.1 %all-to-all-start.13 = ((f32[32,8,128]{2,1,0:T(8,128)}), f32[32,8,128]{2,1,0:T(8,128)S(1)}, u32[]{:S(2)}, u32[]{:S(2)}) async-start(f32[32,8,128]{2,1,0:T(8,128)} %broadcast_in_dim.91), calls=%async_computation.13 | async-start | bytes 262144 | tf_op jit(solution)/shard_map/all_to_all | solution.py:167
  498.6 26.5 %collective-permute-start.24 = (bf16[1,8,1,8,256]{4,3,2,1,0:T(8,128)(2,1)}, bf16[1,8,1,8,256]{4,3,2,1,0:T(8,128)(2,1)S(1)}, u32[]{:S(2)}, u32[]{:S(2)}) collective-permute-start(bf16[1,8,1,8,256]{4,3,2,1,0:T(8,128)(2,1)} %get-tuple-element.298), channel_id=1, source_target_pairs={{0,2},{2,4},{4,6},{1,3},{3,5},{5,7},{8,10},{10,12},{12,14},{9,11},... | collective-permute-start | bytes 98312 | tf_op jit(solution)/shard_map/ppermute | solution.py:28
  502.4 22.8 %collective-permute-start.25 = (bf16[1,8,1,8,256]{4,3,2,1,0:T(8,128)(2,1)S(1)}, bf16[1,8,1,8,256]{4,3,2,1,0:T(8,128)(2,1)S(1)}, u32[]{:S(2)}, u32[]{:S(2)}) collective-permute-start(bf16[1,8,1,8,256]{4,3,2,1,0:T(8,128)(2,1)S(1)} %get-tuple-element.299), channel_id=1, source_target_pairs={{2,0},{4,2},{6,4},{3,1},{5,3},{7,5},{10,8},{12,10},{14,12},{11,9},... | collective-permute-start | bytes 98312 | tf_op jit(solution)/shard_map/ppermute | solution.py:29
  504.0 7.3 collective-permute-start.28
  508.5 6.5 collective-permute-start.29
  532.9 14.6 %all-to-all-start.14 = ((f32[32,8,128]{2,1,0:T(8,128)}), f32[32,8,128]{2,1,0:T(8,128)}, u32[]{:S(2)}, u32[]{:S(2)}) async-start(f32[32,8,128]{2,1,0:T(8,128)} %broadcast_in_dim.93), calls=%async_computation.14 | async-start | bytes 262144 | tf_op jit(solution)/shard_map/all_to_all | solution.py:167
  556.4 28.4 %all-to-all-start.15 = ((f32[32,8,128]{2,1,0:T(8,128)}), f32[32,8,128]{2,1,0:T(8,128)}, u32[]{:S(2)}, u32[]{:S(2)}) async-start(f32[32,8,128]{2,1,0:T(8,128)} %broadcast_in_dim.95), calls=%async_computation.15 | async-start | bytes 262144 | tf_op jit(solution)/shard_map/all_to_all | solution.py:167
  608.3 20.0 %collective-permute-start.32 = (bf16[4,4,1,832,128]{4,3,2,1,0:T(8,128)(2,1)}, bf16[4,4,1,832,128]{4,3,2,1,0:T(8,128)(2,1)}, u32[]{:S(2)}, u32[]{:S(2)}) collective-permute-start(bf16[4,4,1,832,128]{4,3,2,1,0:T(8,128)(2,1)} %constant_dynamic-slice_fusion.9), channel_id=1, source_target_pairs={{0,1},{1,0},{2,3},{3,2},{4,5},{5,4},{6,7},{7,6},{8,9},{9,8},{10,11... | collective-permute-start | bytes 10223624 | tf_op jit(solution)/shard_map/ppermute | solution.py:506
  613.8 40.3 %collective-permute-start.38 = (bf16[4,2,1,832,128]{4,3,2,1,0:T(8,128)(2,1)}, bf16[4,2,1,832,128]{4,3,2,1,0:T(8,128)(2,1)}, u32[]{:S(2)}, u32[]{:S(2)}) collective-permute-start(bf16[4,2,1,832,128]{4,3,2,1,0:T(8,128)(2,1)} %constant_dynamic-slice_fusion.3), channel_id=1, source_target_pairs={{0,4},{2,6},{4,0},{6,2},{1,5},{3,7},{5,1},{7,3},{8,12},{10,14},{12... | collective-permute-start | bytes 5111816 | tf_op jit(solution)/shard_map/ppermute | solution.py:506
  634.8 55.3 %collective-permute-start.33 = (bf16[4,2,1,832,128]{4,3,2,1,0:T(8,128)(2,1)}, bf16[4,2,1,832,128]{4,3,2,1,0:T(8,128)(2,1)}, u32[]{:S(2)}, u32[]{:S(2)}) collective-permute-start(bf16[4,2,1,832,128]{4,3,2,1,0:T(8,128)(2,1)} %constant_dynamic-slice_fusion.8), channel_id=1, source_target_pairs={{0,4},{2,6},{4,0},{6,2},{1,5},{3,7},{5,1},{7,3},{8,12},{10,14},{12... | collective-permute-start | bytes 5111816 | tf_op jit(solution)/shard_map/ppermute | solution.py:506
  658.3 20.1 %collective-permute-start.39 = (bf16[4,1,1,832,128]{4,3,2,1,0:T(8,128)(2,1)}, bf16[4,1,1,832,128]{4,3,2,1,0:T(8,128)(2,1)}, u32[]{:S(2)}, u32[]{:S(2)}) collective-permute-start(bf16[4,1,1,832,128]{4,3,2,1,0:T(8,128)(2,1)} %constant_dynamic-slice_fusion.2), channel_id=1, source_target_pairs={{0,2},{2,0},{4,6},{6,4},{1,3},{3,1},{5,7},{7,5},{8,10},{10,8},{12,... | collective-permute-start | bytes 2555912 | tf_op jit(solution)/shard_map/ppermute | solution.py:506
  692.1 23.6 %collective-permute-start.34 = (bf16[4,1,1,832,128]{4,3,2,1,0:T(8,128)(2,1)S(1)}, bf16[4,1,1,832,128]{4,3,2,1,0:T(8,128)(2,1)S(1)}, u32[]{:S(2)}, u32[]{:S(2)}) collective-permute-start(bf16[4,1,1,832,128]{4,3,2,1,0:T(8,128)(2,1)S(1)} %constant_dynamic-slice_fusion.7), channel_id=1, source_target_pairs={{0,2},{2,0},{4,6},{6,4},{1,3},{3,1},{5,7},{7,5},{8,10},{10,8},{12,... | collective-permute-start | bytes 2555912 | tf_op jit(solution)/shard_map/ppermute | solution.py:506
  693.8 21.1 %collective-permute-start.40 = (bf16[2,1,1,832,128]{4,3,2,1,0:T(8,128)(2,1)S(1)}, bf16[2,1,1,832,128]{4,3,2,1,0:T(8,128)(2,1)S(1)}, u32[]{:S(2)}, u32[]{:S(2)}) collective-permute-start(bf16[2,1,1,832,128]{4,3,2,1,0:T(8,128)(2,1)S(1)} %constant_dynamic-slice_fusion.1), channel_id=1, source_target_pairs={{0,16},{8,24},{16,0},{24,8},{1,17},{9,25},{17,1},{25,9},{2,18},{10... | collective-permute-start | bytes 1277960 | tf_op jit(solution)/shard_map/ppermute | solution.py:506
  715.1 10.3 %collective-permute-start.41 = (bf16[1,1,1,832,128]{4,3,2,1,0:T(8,128)(2,1)S(1)}, bf16[1,1,1,832,128]{4,3,2,1,0:T(8,128)(2,1)S(1)}, u32[]{:S(2)}, u32[]{:S(2)}) collective-permute-start(bf16[1,1,1,832,128]{4,3,2,1,0:T(8,128)(2,1)S(1)} %constant_dynamic-slice_fusion), channel_id=1, source_target_pairs={{0,8},{8,0},{16,24},{24,16},{1,9},{9,1},{17,25},{25,17},{2,10},{10... | collective-permute-start | bytes 638984 | tf_op jit(solution)/shard_map/ppermute | solution.py:506
  715.9 22.3 %collective-permute-start.35 = (bf16[2,1,1,832,128]{4,3,2,1,0:T(8,128)(2,1)S(1)}, bf16[2,1,1,832,128]{4,3,2,1,0:T(8,128)(2,1)S(1)}, u32[]{:S(2)}, u32[]{:S(2)}) collective-permute-start(bf16[2,1,1,832,128]{4,3,2,1,0:T(8,128)(2,1)S(1)} %constant_dynamic-slice_fusion.6), channel_id=1, source_target_pairs={{0,16},{8,24},{16,0},{24,8},{1,17},{9,25},{17,1},{25,9},{2,18},{10... | collective-permute-start | bytes 1277960 | tf_op jit(solution)/shard_map/ppermute | solution.py:506
  738.4 6.4 collective-permute-start.36
  (388 other events, 2921.9 us)
